TPU v7x, 32 devices: a whole 2x2x4 slice. The times are simulated.
32 devices in a mesh: docs: 8 (over z, core), protos: 4 (over y, x).
Axes of the slice: x: 2, y: 2, z: 4, core: 2. Of those that a mesh axis runs over, the one named last changes fastest.
Arguments:
- embeddings: bfloat16 [8192, 512], P('docs'), may hold values from -12.5 to 12.5
- prototypes: bfloat16 [65536, 512], P('protos'), may hold values from -4 to 4
Outputs:
- new_prototypes: bfloat16 [65536, 512], P(('protos', 'docs'))
- column_potential: float32 [65536], P('protos')
- row_potential: float32 [8192], P('docs')
All inputs are finite; a program needn't handle non-finite values.
Results may differ from a plain program's by a relative error of at most 0.0035.
Values may be sent and summed in bfloat16 or wider, within the bound.
No kernel may reach another device: no remote copies, remote signals or barrier semaphores. Data moves between devices by JAX's collectives and lax.ppermute only.
A program may use at most 256 MiB of HBM per device.

v0:
```python
import math
import jax
import jax.numpy as jnp
from jax import lax
from jax.sharding import PartitionSpec as P

SWEEPS = 2


def on_device(embeddings, prototypes):
    local_docs = embeddings.shape[0]
    local_protos = prototypes.shape[0]
    total_docs = local_docs * lax.axis_size("docs")
    total_protos = local_protos * lax.axis_size("protos")
    logit_gain = 4.0 / math.sqrt(embeddings.shape[1])
    scores = (
        lax.dot_general(
            embeddings, prototypes, (((1,), (1,)), ((), ())), preferred_element_type=jnp.float32
        )
        * logit_gain
    )
    row_peak = lax.pmax(jnp.max(scores, axis=1), "protos")
    numerators = jnp.exp(scores - row_peak[:, None])
    row_total = lax.psum(jnp.sum(numerators, axis=1), "protos")
    rescale = 1.0
    row_scale = 1.0 / row_total
    row_weight = rescale * row_scale
    col_scale = jnp.zeros((local_protos,), jnp.float32)
    for sweep_index in range(SWEEPS):
        col_local = jnp.dot(
            row_weight,
            numerators,
            precision=lax.Precision.HIGHEST,
            preferred_element_type=jnp.float32,
        )
        col_total = lax.psum(col_local, "docs")
        col_scale = 1.0 / (total_protos * col_total)
        row_local = rescale * jnp.dot(
            numerators,
            col_scale,
            precision=lax.Precision.HIGHEST,
            preferred_element_type=jnp.float32,
        )
        row_sum = lax.psum(row_local, "protos")
        row_scale = 1.0 / (total_docs * row_sum)
        row_weight = rescale * row_scale
    column_potential = jnp.log(total_docs * col_scale)
    row_potential = jnp.log(row_scale * row_total)
    assignment = (numerators * (total_docs * row_weight)[:, None] * col_scale[None, :]).astype(
        jnp.bfloat16
    )
    summed = lax.psum_scatter(
        lax.dot_general(
            assignment, embeddings, (((0,), (0,)), ((), ())), preferred_element_type=jnp.float32
        ),
        "docs",
        scatter_dimension=0,
        tiled=True,
    )
    new_prototypes = (
        summed * lax.rsqrt(jnp.mean(summed * summed, axis=1, keepdims=True) + 1e-06)
    ).astype(jnp.bfloat16)
    return (new_prototypes, column_potential, row_potential)


def solution(mesh):
    placed = (P("docs", None), P("protos", None))
    return jax.shard_map(
        on_device,
        mesh=mesh,
        in_specs=placed,
        out_specs=(P(("protos", "docs"), None), P("protos"), P("docs")),
        check_vma=False,
    )
```

profile of v0, /device:TPU:0, one launch (start us, length us, event | category | flops | bytes accessed | tf_op | source)
XLA Modules:
  0.0 816.3 jit_solution(17064669797004932549)
XLA Ops:
  7.2 0.0 copy-start
  7.2 0.0 all-reduce.3.cloned.1.call-start
  7.2 1.2 copy-done
  8.4 31.5 %multiply_reduce_fusion = (f32[1024]{0:T(1024)S(1)}, f32[1024,16384]{1,0:T(8,128)}) fusion(bf16[1024,512]{1,0:T(8,128)(2,1)S(1)} %copy-done, bf16[16384,512]{1,0:T(8,128)(2,1)} %param.3), kind=kOutput, calls=%fused_computation.2 | convolution fusion | flops 17213423616 | bytes 84938752 | tf_op jit(solution)/shard_map/dot_general | solution.py:17
  39.9 11.3 %pmax.7 = f32[1024]{0:T(1024)S(1)} all-reduce(f32[1024]{0:T(1024)S(1)} %get-tuple-element.7), channel_id=1, replica_groups=mesh['docs'=8,'protos'=4] {'protos'}, use_global_device_ids=true, to_apply=%region_1.0 | all-reduce | flops 1024 | bytes 8192 | tf_op jit(solution)/shard_map/pmax | solution.py:22
  51.2 21.2 %fusion.7 = f32[1024]{0:T(1024)S(1)} fusion(f32[1024]{0:T(1024)S(1)} %pmax.7, f32[1024,16384]{1,0:T(8,128)} %get-tuple-element.8), kind=kLoop, calls=%fused_computation.21 | loop fusion | flops 50330624 | bytes 67117056 | tf_op jit(solution)/shard_map/reduce_sum | solution.py:24
  72.4 8.3 %psum.35 = f32[1024]{0:T(1024)S(1)} all-reduce(f32[1024]{0:T(1024)S(1)} %fusion.7), channel_id=1, replica_groups=mesh['docs'=8,'protos'=4] {'protos'}, use_global_device_ids=true, to_apply=%region_3.0 | all-reduce | flops 1024 | bytes 8192 | tf_op jit(solution)/shard_map/psum | solution.py:24
  80.7 46.4 %fusion.6 = f32[1,16384]{1,0:T(1,128)} fusion(f32[1024,1]{0,1:T(1,128)S(1)} %bitcast.20, f32[1024,16384]{1,0:T(8,128)} %get-tuple-element.8, f32[1024]{0:T(1024)S(1)} %pmax.7), kind=kOutput, calls=%fused_computation.20 | convolution fusion | flops 234881024 | bytes 67182592 | tf_op jit(solution)/shard_map/dot_general | solution.py:30
  127.1 0.0 all-reduce.3.cloned.1.call-update
  127.1 0.6 all-reduce.5.cloned.1.call-start
  127.8 53.4 %all-reduce.3.cloned.1.call-done = f32[16384]{0:T(1024)} async-done(((f32[16384]{0:T(1024)}), f32[16384]{0:T(1024)}) %all-reduce.3.cloned.1.call-update) | async-done | bytes 65552 | tf_op jit(solution)/shard_map/psum | solution.py:36
  181.2 0.9 multiply_divide_fusion.1
  182.1 69.4 %fusion.5 = f32[1,1024]{1,0:T(1,128)S(1)} fusion(f32[16384,1]{0,1:T(1,128)S(1)} %bitcast.16, f32[1024,16384]{1,0:T(8,128)} %get-tuple-element.8, f32[1024]{0:T(1024)S(1)} %pmax.7), kind=kOutput, calls=%fused_computation.19 | convolution fusion | flops 234881024 | bytes 67182592 | tf_op jit(solution)/shard_map/dot_general | solution.py:38
  251.5 10.0 %psum.37 = f32[1024]{0:T(1024)S(1)} all-reduce(f32[1024]{0:T(1024)S(1)} %bitcast.21), channel_id=1, replica_groups=mesh['docs'=8,'protos'=4] {'protos'}, use_global_device_ids=true, to_apply=%region_5.0 | all-reduce | flops 1024 | bytes 8192 | tf_op jit(solution)/shard_map/psum | solution.py:44
  261.5 46.4 %fusion.4 = f32[1,16384]{1,0:T(1,128)} fusion(f32[1024,1]{0,1:T(1,128)S(1)} %bitcast.19, f32[1024,16384]{1,0:T(8,128)} %get-tuple-element.8, f32[1024]{0:T(1024)S(1)} %pmax.7), kind=kOutput, calls=%fused_computation.18 | convolution fusion | flops 234881024 | bytes 67182592 | tf_op jit(solution)/shard_map/dot_general | solution.py:30
  307.9 0.0 all-reduce.5.cloned.1.call-update
  307.9 0.3 reduce-scatter.2.cloned.1.call-start
  308.1 50.7 %all-reduce.5.cloned.1.call-done = f32[16384]{0:T(1024)} async-done(((f32[16384]{0:T(1024)}), f32[16384]{0:T(1024)}) %all-reduce.5.cloned.1.call-update) | async-done | bytes 65552 | tf_op jit(solution)/shard_map/psum | solution.py:36
  358.8 1.5 multiply_log_fusion
  360.3 69.4 %fusion.3 = f32[1,1024]{1,0:T(1,128)S(1)} fusion(f32[16384,1]{0,1:T(1,128)S(1)} %bitcast.15, f32[1024,16384]{1,0:T(8,128)} %get-tuple-element.8, f32[1024]{0:T(1024)S(1)} %pmax.7), kind=kOutput, calls=%fused_computation.17 | convolution fusion | flops 234881024 | bytes 67182592 | tf_op jit(solution)/shard_map/dot_general | solution.py:38
  429.7 10.1 %psum.39 = f32[1024]{0:T(1024)S(1)} all-reduce(f32[1024]{0:T(1024)S(1)} %bitcast.22), channel_id=1, replica_groups=mesh['docs'=8,'protos'=4] {'protos'}, use_global_device_ids=true, to_apply=%region_7.0 | all-reduce | flops 1024 | bytes 8192 | tf_op jit(solution)/shard_map/psum | solution.py:44
  439.8 0.6 multiply_log_fusion.1
  440.4 39.8 %fusion = f32[16384,512]{1,0:T(8,128)} fusion(bf16[1024,512]{1,0:T(8,128)(2,1)S(1)} %copy-done, f32[16384]{0:T(1024)S(1)} %get-tuple-element.4, f32[1024]{0:T(1024)S(1)} %get-tuple-element.6, f32[1024,16384]{1,0:T(8,128)} %get-tuple-element.8, f32[1024]{0:T(1024)S(1)} %pmax.7), kind=kOutput, calls=%fused_computation.3 | convolution fusion | flops 17263755264 | bytes 101785600 | tf_op jit(solution)/shard_map/dot_general | solution.py:53
  480.2 0.0 reduce-scatter.2.cloned.1.call-update
  480.2 322.9 %reduce-scatter.2.cloned.1.call-done = f32[2048,512]{1,0:T(8,128)} async-done(((f32[16384,512]{1,0:T(8,128)}), f32[2048,512]{1,0:T(8,128)}) %reduce-scatter.2.cloned.1.call-update) | async-done | bytes 4194320 | tf_op jit(solution)/shard_map/reduce_scatter | solution.py:52
  803.1 2.5 multiply_reduce_fusion.1
  805.7 3.8 multiply_convert_fusion.2
  (3 shorter events, 0.0 us)
Async XLA Ops:
  7.2 1.2 copy-start
  7.2 174.0 %all-reduce.3.cloned.1.call-start = ((), (), s32[]{:S(2)}) async-start(), calls=%async_computation.1 | async-start | bytes 131072 | tf_op jit(solution)/shard_map/psum | solution.py:36
  127.1 231.7 %all-reduce.5.cloned.1.call-start = ((), (), s32[]{:S(2)}) async-start(), calls=%async_computation.2 | async-start | bytes 131072 | tf_op jit(solution)/shard_map/psum | solution.py:36
  307.9 495.2 %reduce-scatter.2.cloned.1.call-start = ((), (), s32[]{:S(2)}) async-start(), calls=%async_computation.3 | async-start | bytes 37748736 | tf_op jit(solution)/shard_map/reduce_scatter | solution.py:52
Sparse Core Ops, SparseCore 0:
  127.3 53.9 all-reduce.2
  308.0 50.7 all-reduce.4
  480.4 322.6 reduce-scatter.1
where the time goes:
time: 820 us; the launch traced here: 816 us
  waiting for transfers between devices  427 us (52%)
  matrix products  303 us (37%)
  blocking collectives  39.7 us (5%)
  other arithmetic  30.6 us (4%)
  between operations  14.1 us (2%)
    reduce_scatter x1, waiting for transfers between devices, on_device(): lax.psum_scatter(lax.dot_general(assignment, embeddings, (((0,), (0,)), (...  323 us
    dot_general x2, matrix products, on_device(): jnp.dot(numerators, col_scale, precision=lax.Precision.HIGHEST, preferred...  139 us
    psum x2, waiting for transfers between devices, on_device(): col_total = lax.psum(col_local, 'docs')  104 us
    dot_general x2, matrix products, on_device(): jnp.dot(row_weight, numerators, precision=lax.Precision.HIGHEST, preferre...  92.8 us
    dot_general x1, matrix products, on_device(): lax.dot_general(assignment, embeddings, (((0,), (0,)), ((), ())), preferr...  39.8 us
    dot_general x1, matrix products, on_device(): lax.dot_general(embeddings, prototypes, (((1,), (1,)), ((), ())), preferr...  31.5 us
    reduce_sum x1, other arithmetic, on_device(): row_total = lax.psum(jnp.sum(numerators, axis=1), 'protos')  21.2 us
    psum x2, blocking collectives, on_device(): row_sum = lax.psum(row_local, 'protos')  20.1 us
  transfers between devices with their start and end apart: 3, of which 3 were waited for; matrix products, arithmetic and copies ran while one was open for 0% of the time, Pallas kernels for 0%

commit v1 on v0

--- a/solution.py
+++ b/solution.py
@@ -33,7 +33,11 @@
             precision=lax.Precision.HIGHEST,
             preferred_element_type=jnp.float32,
         )
-        col_total = lax.psum(col_local, "docs")
+
+        def _make_regions(my_tile):
+            return jnp.sum(jax.lax.all_gather(my_tile, axis_name="docs"), axis=0)
+
+        col_total = _make_regions(col_local)
         col_scale = 1.0 / (total_protos * col_total)
         row_local = rescale * jnp.dot(
             numerators,

time: 820 us -> 745 us (0.909)
  waiting for transfers between devices: 427 us -> 326 us
  blocking collectives: 39.7 us -> 68.1 us
    psum x2 -> x0, waiting for transfers between devices: 104 us -> none  [on_device(): col_total = lax.psum(col_local, 'docs')]
    all_gather x0 -> x2, blocking collectives: none -> 30.9 us  [_make_regions(): return jnp.sum(jax.lax.all_gather(my_tile, axis_name='docs'), axis=0)]
  transfers between devices with their start and end apart: 3 -> 1, of which waited for: 3 -> 1; matrix products, arithmetic and copies ran while one was open for 0% -> 0% of each run, Pallas kernels for 0% -> 0%
where the time goes in v1:
time: 745 us; the launch traced here: 741 us
  waiting for transfers between devices  326 us (44%)
  matrix products  302 us (41%)
  blocking collectives  68.1 us (9%)
  other arithmetic  29.2 us (4%)
  between operations  14.6 us (2%)
    reduce_scatter x1, waiting for transfers between devices, on_device(): lax.psum_scatter(lax.dot_general(assignment, embeddings, (((0,), (0,)), (...  326 us
    dot_general x2, matrix products, on_device(): jnp.dot(numerators, col_scale, precision=lax.Precision.HIGHEST, preferred...  139 us
    dot_general x2, matrix products, on_device(): jnp.dot(row_weight, numerators, precision=lax.Precision.HIGHEST, preferre...  91.5 us
    dot_general x1, matrix products, on_device(): lax.dot_general(assignment, embeddings, (((0,), (0,)), ((), ())), preferr...  39.8 us
    dot_general x1, matrix products, on_device(): lax.dot_general(embeddings, prototypes, (((1,), (1,)), ((), ())), preferr...  31.5 us
    all_gather x2, blocking collectives, _make_regions(): return jnp.sum(jax.lax.all_gather(my_tile, axis_name='docs'), axis=0)  30.9 us
    reduce_sum x1, other arithmetic, on_device(): row_total = lax.psum(jnp.sum(numerators, axis=1), 'protos')  21.2 us
    psum x2, blocking collectives, on_device(): row_sum = lax.psum(row_local, 'protos')  17.4 us
  transfers between devices with their start and end apart: 1, of which 1 were waited for; matrix products, arithmetic and copies ran while one was open for 0% of the time, Pallas kernels for 0%

profile of v1, /device:TPU:0, one launch (start us, length us, event | category | flops | bytes accessed | tf_op | source)
XLA Modules:
  0.0 741.1 jit_solution(15374560166229347792)
XLA Ops:
  7.2 0.0 copy-start
  7.2 0.0 reduce-scatter.2.cloned.1.call-start
  7.2 1.2 copy-done
  8.4 31.5 %multiply_reduce_fusion = (f32[1024]{0:T(1024)S(1)}, f32[1024,16384]{1,0:T(8,128)}) fusion(bf16[1024,512]{1,0:T(8,128)(2,1)S(1)} %copy-done, bf16[16384,512]{1,0:T(8,128)(2,1)} %param.3), kind=kOutput, calls=%fused_computation.2 | convolution fusion | flops 17213423616 | bytes 84938752 | tf_op jit(solution)/shard_map/dot_general | solution.py:17
  39.9 11.3 %pmax.7 = f32[1024]{0:T(1024)S(1)} all-reduce(f32[1024]{0:T(1024)S(1)} %get-tuple-element.7), channel_id=1, replica_groups=mesh['docs'=8,'protos'=4] {'protos'}, use_global_device_ids=true, to_apply=%region_1.0 | all-reduce | flops 1024 | bytes 8192 | tf_op jit(solution)/shard_map/pmax | solution.py:22
  51.2 21.2 %fusion.7 = f32[1024]{0:T(1024)S(1)} fusion(f32[1024]{0:T(1024)S(1)} %pmax.7, f32[1024,16384]{1,0:T(8,128)} %get-tuple-element.8), kind=kLoop, calls=%fused_computation.21 | loop fusion | flops 50330624 | bytes 67117056 | tf_op jit(solution)/shard_map/reduce_sum | solution.py:24
  72.4 8.5 %psum.21 = f32[1024]{0:T(1024)S(1)} all-reduce(f32[1024]{0:T(1024)S(1)} %fusion.7), channel_id=1, replica_groups=mesh['docs'=8,'protos'=4] {'protos'}, use_global_device_ids=true, to_apply=%region_3.0 | all-reduce | flops 1024 | bytes 8192 | tf_op jit(solution)/shard_map/psum | solution.py:24
  80.9 45.8 %fusion.6 = f32[1,16384]{1,0:T(1,128)S(1)} fusion(f32[1024,1]{0,1:T(1,128)S(1)} %bitcast.20, f32[1024,16384]{1,0:T(8,128)} %get-tuple-element.8, f32[1024]{0:T(1024)S(1)} %pmax.7), kind=kOutput, calls=%fused_computation.20 | convolution fusion | flops 234881024 | bytes 67182592 | tf_op jit(solution)/shard_map/dot_general | solution.py:30
  126.7 15.6 %all-gather = f32[131072]{0:T(1024)S(1)} all-gather(f32[16384]{0:T(1024)S(1)} %bitcast.17), channel_id=2, replica_groups=mesh['docs'=8,'protos'=4] {'docs'}, dimensions={0}, use_global_device_ids=true | all-gather | bytes 589824 | tf_op jit(solution)/shard_map/all_gather | solution.py:38
  142.3 0.1 reshape.20
  142.4 0.1 reduce_sum.37
  142.5 69.4 %fusion.5 = f32[1,1024]{1,0:T(1,128)S(1)} fusion(f32[16384,1]{0,1:T(1,128)S(1)} %bitcast.16, f32[1024,16384]{1,0:T(8,128)} %get-tuple-element.8, f32[1024]{0:T(1024)S(1)} %pmax.7), kind=kOutput, calls=%fused_computation.19 | convolution fusion | flops 234881024 | bytes 67182592 | tf_op jit(solution)/shard_map/dot_general | solution.py:42
  211.9 9.2 %psum.22 = f32[1024]{0:T(1024)S(1)} all-reduce(f32[1024]{0:T(1024)S(1)} %bitcast.21), channel_id=1, replica_groups=mesh['docs'=8,'protos'=4] {'protos'}, use_global_device_ids=true, to_apply=%region_5.0 | all-reduce | flops 1024 | bytes 8192 | tf_op jit(solution)/shard_map/psum | solution.py:48
  221.1 45.8 %fusion.4 = f32[1,16384]{1,0:T(1,128)S(1)} fusion(f32[1024,1]{0,1:T(1,128)S(1)} %bitcast.19, f32[1024,16384]{1,0:T(8,128)} %get-tuple-element.8, f32[1024]{0:T(1024)S(1)} %pmax.7), kind=kOutput, calls=%fused_computation.18 | convolution fusion | flops 234881024 | bytes 67182592 | tf_op jit(solution)/shard_map/dot_general | solution.py:30
  266.9 15.3 %all-gather.1 = f32[131072]{0:T(1024)S(1)} all-gather(f32[16384]{0:T(1024)S(1)} %bitcast.18), channel_id=3, replica_groups=mesh['docs'=8,'protos'=4] {'docs'}, dimensions={0}, use_global_device_ids=true | all-gather | bytes 589824 | tf_op jit(solution)/shard_map/all_gather | solution.py:38
  282.1 0.1 reshape.21
  282.2 0.1 reduce_sum.38
  282.4 0.7 multiply_log_fusion
  283.0 69.4 %fusion.3 = f32[1,1024]{1,0:T(1,128)S(1)} fusion(f32[16384,1]{0,1:T(1,128)S(1)} %bitcast.15, f32[1024,16384]{1,0:T(8,128)} %get-tuple-element.8, f32[1024]{0:T(1024)S(1)} %pmax.7), kind=kOutput, calls=%fused_computation.17 | convolution fusion | flops 234881024 | bytes 67182592 | tf_op jit(solution)/shard_map/dot_general | solution.py:42
  352.4 8.3 %psum.23 = f32[1024]{0:T(1024)S(1)} all-reduce(f32[1024]{0:T(1024)S(1)} %bitcast.22), channel_id=1, replica_groups=mesh['docs'=8,'protos'=4] {'protos'}, use_global_device_ids=true, to_apply=%region_7.0 | all-reduce | flops 1024 | bytes 8192 | tf_op jit(solution)/shard_map/psum | solution.py:48
  360.7 0.6 multiply_log_fusion.1
  361.3 39.8 %fusion = f32[16384,512]{1,0:T(8,128)} fusion(bf16[1024,512]{1,0:T(8,128)(2,1)S(1)} %copy-done, f32[16384]{0:T(1024)S(1)} %get-tuple-element.4, f32[1024]{0:T(1024)S(1)} %get-tuple-element.6, f32[1024,16384]{1,0:T(8,128)} %get-tuple-element.8, f32[1024]{0:T(1024)S(1)} %pmax.7), kind=kOutput, calls=%fused_computation.3 | convolution fusion | flops 17263755264 | bytes 101785600 | tf_op jit(solution)/shard_map/dot_general | solution.py:57
  401.1 0.0 reduce-scatter.2.cloned.1.call-update
  401.1 326.3 %reduce-scatter.2.cloned.1.call-done = f32[2048,512]{1,0:T(8,128)} async-done(((f32[16384,512]{1,0:T(8,128)}), f32[2048,512]{1,0:T(8,128)}) %reduce-scatter.2.cloned.1.call-update) | async-done | bytes 4194320 | tf_op jit(solution)/shard_map/reduce_scatter | solution.py:56
  727.4 2.5 multiply_reduce_fusion.1
  729.9 3.8 multiply_convert_fusion.2
  (4 shorter events, 0.0 us)
Async XLA Ops:
  7.2 1.2 copy-start
  7.2 720.2 %reduce-scatter.2.cloned.1.call-start = ((), (), s32[]{:S(2)}) async-start(), calls=%async_computation.1 | async-start | bytes 37748736 | tf_op jit(solution)/shard_map/reduce_scatter | solution.py:56
Sparse Core Ops, SparseCore 0:
  401.2 326.1 reduce-scatter.1
